TPU v7x, 32 devices: a whole 2x2x4 slice. The times are simulated.
32 devices in a mesh: grp: 8 (over z, x), tp: 4 (over y, core).
Axes of the slice: x: 2, y: 2, z: 4, core: 2. Of those that a mesh axis runs over, the one named last changes fastest.
Arguments:
- thinker_rows: bfloat16 [2048, 8192], P(('grp', 'tp')), may hold values from -6 to 6
- norm_gain: bfloat16 [8192], replicated, may hold values from 0.5 to 1.5
- w_query: bfloat16 [8192, 4096], P(None, 'tp'), may hold values from -0.0625 to 0.0625
- w_key: bfloat16 [8192, 1024], P(None, 'tp'), may hold values from -0.0625 to 0.0625
- w_value: bfloat16 [8192, 1024], P(None, 'tp'), may hold values from -0.0625 to 0.0625
- w_out: bfloat16 [4096, 8192], P('tp'), may hold values from -0.75 to 0.75
- cache_keys: bfloat16 [128, 320, 1024], P('grp', None, 'tp'), may hold values from -576 to 576
- cache_values: bfloat16 [128, 320, 1024], P('grp', None, 'tp'), may hold values from -6 to 6
- session_ids: int32 [8, 256], P('grp'), may hold values from 0 to 15, never falling along the last dimension, each value on 1 to 20 neighbouring positions
- cache_lens: int32 [8, 16], P('grp'), may hold values from 1 to 320, 3200 in all within a row
- owners: int32 [128, 1], P('grp'), may hold values from 0 to 7; in each aligned block of 16 rows (0 to 15, 16 to 31, ...) at most 2 rows name the same one
- talker_gain: bfloat16 [8192], replicated, may hold values from 0.5 to 1.5
- w_talker: bfloat16 [8192, 1024], P(None, 'tp'), may hold values from -0.0625 to 0.0625
Outputs:
- talker_rows: bfloat16 [2560, 1024], P('grp', 'tp')
Inputs may be any that keep to these rules, and one draw needn't show every extreme that they name: `session_ids`: within a group the ids never fall; every one of the 16 sessions has 1 to 20 tokens and some session exactly 20. `cache_lens`: some session of every group has exactly 320 live slots. `owners`: of one group's 16 sessions at most 2 have the same owner, and some owner has exactly 2 of some group.
All inputs are finite; a program needn't handle non-finite values.
Results may differ from a plain program's by a relative error of at most 0.017.
The roundings to bfloat16 on the way count: a program that leaves them out, or rounds other values in their place, can miss the bound.
Values may be sent and summed in bfloat16 or wider, within the bound.
A program may use at most 128 MiB of HBM per device.

v0:
```python
import jax
import jax.numpy as jnp
from jax import lax
from jax.sharding import PartitionSpec as P

HEAD_DIM = 128
SESS = 16
CAPS = 2
GQA = 4
MOST = 20


EPSILON = 1e-06


def rms_scaled(values, weights):
    floats = values.astype(jnp.float32)
    mean_square = jnp.mean(floats * floats, axis=-1, keepdims=True)
    return (floats * lax.rsqrt(mean_square + EPSILON) * weights.astype(jnp.float32)).astype(
        jnp.bfloat16
    )


def slot_tables(session_row, owner_row):
    session_range = jnp.arange(SESS, dtype=jnp.int32)
    member = (session_row[:, None] == session_range[None, :]).astype(jnp.int32)
    counts = jnp.sum(member, axis=0)
    starts = jnp.cumsum(counts) - counts
    first_row = jnp.sum(member * starts[None, :], axis=1)
    position = jnp.arange(session_row.shape[0], dtype=jnp.int32) - first_row
    earlier = (owner_row[:, None] == owner_row[None, :]) & (
        session_range[None, :] < session_range[:, None]
    )
    owner_rank = jnp.sum(earlier.astype(jnp.int32), axis=1)
    owner_slot = owner_row * CAPS + owner_rank
    destination = jnp.sum(member * owner_slot[None, :], axis=1) * MOST + position
    slot_index = session_row * MOST + position
    return (counts, slot_index, destination)


def attend(q_slots, k_slots, v_slots, cache_k, cache_v, live_lens, counts):
    score_scale = HEAD_DIM ** (-0.5)
    cached = (
        jnp.einsum("smkgd,sckd->skgmc", q_slots, cache_k, preferred_element_type=jnp.float32)
        * score_scale
    )
    fresh = (
        jnp.einsum("smkgd,snkd->skgmn", q_slots, k_slots, preferred_element_type=jnp.float32)
        * score_scale
    )
    live_cache = jnp.arange(cache_k.shape[1], dtype=jnp.int32)[None, :] < live_lens[:, None]
    places = jnp.arange(MOST, dtype=jnp.int32)
    causal = places[None, :] <= places[:, None]
    live_fresh = causal[None, :, :] & (places[None, None, :] < counts[:, None, None])
    cached = jnp.where(live_cache[:, None, None, None, :], cached, -1e30)
    fresh = jnp.where(live_fresh[:, None, None, :, :], fresh, -1e30)
    highest = jnp.maximum(jnp.max(cached, axis=-1), jnp.max(fresh, axis=-1))
    exp_cached = jnp.exp(cached - highest[..., None])
    exp_fresh = jnp.exp(fresh - highest[..., None])
    denominator = jnp.sum(exp_cached, axis=-1) + jnp.sum(exp_fresh, axis=-1)
    weight_cached = (exp_cached / denominator[..., None]).astype(jnp.bfloat16)
    weight_fresh = (exp_fresh / denominator[..., None]).astype(jnp.bfloat16)
    mixed = jnp.einsum(
        "skgmc,sckd->smkgd", weight_cached, cache_v, preferred_element_type=jnp.float32
    )
    mixed = mixed + jnp.einsum(
        "skgmn,snkd->smkgd", weight_fresh, v_slots, preferred_element_type=jnp.float32
    )
    return mixed.astype(jnp.bfloat16)


def on_device(
    thinker_rows,
    norm_gain,
    w_query,
    w_key,
    w_value,
    w_out,
    cache_keys,
    cache_values,
    session_ids,
    cache_lens,
    owners,
    talker_gain,
    w_talker,
):
    model_width = thinker_rows.shape[1]
    kv_local = w_key.shape[1] // HEAD_DIM
    head_width = GQA * HEAD_DIM
    slot_count = SESS * MOST
    owner_count = lax.axis_size("grp")
    gathered = lax.all_gather(thinker_rows, "tp", axis=0, tiled=True)
    normed = rms_scaled(gathered, norm_gain)
    query = jnp.dot(normed, w_query, preferred_element_type=jnp.float32).astype(jnp.bfloat16)
    key_new = jnp.dot(normed, w_key, preferred_element_type=jnp.float32).astype(jnp.bfloat16)
    value_new = jnp.dot(normed, w_value, preferred_element_type=jnp.float32).astype(jnp.bfloat16)
    counts, slot_index, destination = slot_tables(session_ids[0], owners[:, 0])
    placing = (slot_index[None, :] == jnp.arange(slot_count, dtype=jnp.int32)[:, None]).astype(
        jnp.bfloat16
    )
    q_slots = jnp.dot(placing, query, preferred_element_type=jnp.float32).astype(jnp.bfloat16)
    k_slots = jnp.dot(placing, key_new, preferred_element_type=jnp.float32).astype(jnp.bfloat16)
    v_slots = jnp.dot(placing, value_new, preferred_element_type=jnp.float32).astype(jnp.bfloat16)
    mixed = attend(
        q_slots.reshape(SESS, MOST, kv_local, GQA, HEAD_DIM),
        k_slots.reshape(SESS, MOST, kv_local, HEAD_DIM),
        v_slots.reshape(SESS, MOST, kv_local, HEAD_DIM),
        cache_keys.reshape(SESS, cache_keys.shape[1], kv_local, HEAD_DIM),
        cache_values.reshape(SESS, cache_values.shape[1], kv_local, HEAD_DIM),
        cache_lens[0],
        counts,
    )
    attention_rows = lax.dot_general(
        placing,
        mixed.reshape(slot_count, kv_local * head_width),
        (((0,), (0,)), ((), ())),
        preferred_element_type=jnp.float32,
    ).astype(jnp.bfloat16)
    routing = (
        destination[None, :] == jnp.arange(owner_count * CAPS * MOST, dtype=jnp.int32)[:, None]
    ).astype(jnp.bfloat16)
    head_total = jnp.zeros((gathered.shape[0], model_width), jnp.float32)
    for kv_index in range(kv_local):
        lower = kv_index * head_width
        partial_sum = jnp.dot(
            attention_rows[:, lower : lower + head_width],
            w_out[lower : lower + head_width],
            preferred_element_type=jnp.float32,
        ).astype(jnp.bfloat16)
        head_total = head_total + partial_sum.astype(jnp.float32)
    summed = lax.psum_scatter(
        head_total.astype(jnp.bfloat16), "tp", scatter_dimension=1, tiled=True
    ).astype(jnp.float32)
    share = summed.shape[1]
    residual = lax.dynamic_slice_in_dim(gathered, lax.axis_index("tp") * share, share, 1)
    hidden = (residual.astype(jnp.float32) + summed).astype(jnp.bfloat16)
    outgoing = (
        jnp.dot(routing, hidden, preferred_element_type=jnp.float32)
        .astype(jnp.bfloat16)
        .reshape(owner_count, CAPS * MOST, share)
    )
    arrived = lax.all_to_all(outgoing, "grp", split_axis=0, concat_axis=0, tiled=True)
    arrived_rows = lax.all_gather(
        arrived.reshape(owner_count * CAPS * MOST, share), "tp", axis=1, tiled=True
    )
    return jnp.dot(
        rms_scaled(arrived_rows, talker_gain), w_talker, preferred_element_type=jnp.float32
    ).astype(jnp.bfloat16)


def solution(mesh):
    return jax.shard_map(
        on_device,
        mesh=mesh,
        in_specs=(
            P(("grp", "tp"), None),
            P(),
            P(None, "tp"),
            P(None, "tp"),
            P(None, "tp"),
            P("tp", None),
            P("grp", None, "tp"),
            P("grp", None, "tp"),
            P("grp", None),
            P("grp", None),
            P("grp", None),
            P(),
            P(None, "tp"),
        ),
        out_specs=P("grp", "tp"),
        check_vma=False,
    )
```

profile of v0, /device:TPU:0, one launch (start us, length us, event | category | flops | bytes accessed | tf_op | source)
XLA Modules:
  0.0 238.4 jit_solution(1696441224001356427)
XLA Ops:
  6.5 0.7 all-gather.3.cloned.1.call-update
  7.3 0.8 convert_reduce_fusion
  8.4 0.7 convert_element_type.90
  9.1 4.9 %reshape.167 = bf16[16,320,2,128]{3,2,1,0:T(2,128)(2,1)} reshape(bf16[16,320,256]{2,1,0:T(8,128)(2,1)} %param.19) | data formatting | bytes 5242880 | tf_op jit(solution)/shard_map/reshape | solution.py:108
  14.1 2.8 %reshape.169 = bf16[16,320,2,128]{3,2,1,0:T(2,128)(2,1)} reshape(bf16[16,320,256]{2,1,0:T(8,128)(2,1)S(1)} %copy-done.3) | data formatting | bytes 5242880 | tf_op jit(solution)/shard_map/reshape | solution.py:109
  16.9 0.2 convert_reduce_fusion.1
  17.5 28.6 %all-gather.3.cloned.1.call-done = bf16[256,8192]{1,0:T(8,128)(2,1)} async-done(((bf16[64,8192]{1,0:T(8,128)(2,1)}), bf16[256,8192]{1,0:T(8,128)(2,1)}) %all-gather.3.cloned.1.call-update) | async-done | bytes 4194320 | tf_op jit(solution)/shard_map/all_gather | solution.py:92
  46.1 3.1 %fusion.7 = f32[256]{0:T(256)S(1)} fusion(bf16[256,8192]{1,0:T(8,128)(2,1)} %all-gather.3.cloned.1.call-done), kind=kLoop, calls=%fused_computation.13 | loop fusion | flops 6291200 | bytes 4195328 | tf_op jit(solution)/shard_map/reduce_sum | solution.py:18
  49.2 11.8 %convolution_convert_fusion.3 = bf16[320,1024]{1,0:T(8,128)(2,1)S(1)} fusion(bf16[8192,1024]{1,0:T(8,128)(2,1)} %param.15, s32[256]{0:T(256)S(1)} %bitcast.47, bf16[256,8192]{1,0:T(8,128)(2,1)} %all-gather.3.cloned.1.call-done, f32[8192]{0:T(1024)S(1)} %convert_element_type.90, f32[256]{0:T(256)S(1)} %add_rsqrt_fusion.1), kind=kOutput, calls=%fused_computation.40 | convolution fusion | flops 4471799808 | bytes 21661696 | tf_op jit(solution)/shard_map/dot_general | solution.py:101
  61.1 0.5 reshape.166
  61.5 5.0 %convolution_convert_fusion.7 = bf16[320,256]{1,0:T(8,128)(2,1)S(1)} fusion(bf16[8192,256]{1,0:T(8,128)(2,1)} %param.16, s32[256]{0:T(256)S(1)} %bitcast.48, bf16[256,8192]{1,0:T(8,128)(2,1)} %all-gather.3.cloned.1.call-done, f32[8192]{0:T(1024)S(1)} %convert_element_type.90, f32[256]{0:T(256)S(1)} %add_rsqrt_fusion.1), kind=kOutput, calls=%fused_computation.44 | convolution fusion | flops 1124302848 | bytes 8587264 | tf_op jit(solution)/shard_map/dot_general | solution.py:102
  66.6 1.5 fusion.53
  68.1 3.5 %bitcast_reduce_fusion = (f32[16,2,4,20]{3,2,1,0:T(4,128)S(1)}, f32[16,2,20,4,320]{4,2,3,1,0:T(8,128)S(1)}) fusion(pred[16,320]{1,0:T(8,128)(4,1)S(1)} %iota_compare_fusion.7, bf16[16,320,2,128,1]{3,2,1,0,4:T(2,128)(2,1)} %bitcast.41, bf16[16,20,2,4,128]{4,3,2,1,0:T(4,128)(2,1)S(1)} %reshape.166), kind=kOutput, calls=%fused_computation.22 | convolution fusion | flops 212170240 | bytes 6568960 | tf_op jit(solution)/shard_map/smkgd,sckd->skgmc/dot_general | solution.py:44
  71.7 0.5 fusion.26
  72.1 1.6 copy-done.1
  73.7 1.7 fusion.17
  75.5 5.0 %convolution_convert_fusion.6 = bf16[320,256]{1,0:T(8,128)(2,1)S(1)} fusion(bf16[8192,256]{1,0:T(8,128)(2,1)} %param.17, s32[256]{0:T(256)S(1)} %bitcast.49, bf16[256,8192]{1,0:T(8,128)(2,1)} %all-gather.3.cloned.1.call-done, f32[8192]{0:T(1024)S(1)} %convert_element_type.90, f32[256]{0:T(256)S(1)} %add_rsqrt_fusion.1), kind=kOutput, calls=%fused_computation.43 | convolution fusion | flops 1124302848 | bytes 8587264 | tf_op jit(solution)/shard_map/dot_general | solution.py:103
  80.5 0.5 fusion.31
  81.1 1.8 copy-done.2
  82.8 3.3 %fusion.23 = bf16[16,20,2,4,128]{4,1,3,2,0:T(8,128)(2,1)S(1)} fusion(f32[16,2,128,4,20]{2,4,3,1,0:T(8,128)S(1)} %fusion.31, bf16[16,320,2,128,1]{3,2,1,0,4:T(2,128)(2,1)} %bitcast.40, f32[16,2,20,4,320]{4,2,3,1,0:T(8,128)S(1)} %copy-done.2, f32[16,2,4,20]{3,2,1,0:T(4,128)S(1)} %add.67, f32[16,2,4,20]{3,2,1,0:T(4,128)S(1)} %max.7, ...), kind=kOutput, calls=%fused_computation.35 | convolution fusion | flops 214466560 | bytes 7889920 | tf_op jit(solution)/shard_map/skgmc,sckd->smkgd/dot_general | solution.py:63
  86.2 0.3 copy.39
  86.4 0.5 reshape.171
  86.9 0.5 convolution_convert_fusion.4
  87.4 5.7 %fusion.6 = f32[256,8192]{1,0:T(8,128)S(1)} fusion(bf16[1024,8192]{1,0:T(8,128)(2,1)} %param.18, bf16[256,1024]{1,0:T(8,128)(2,1)S(1)} %convolution_convert_fusion.4), kind=kOutput, calls=%fused_computation.12 | convolution fusion | flops 2151677952 | bytes 17039360 | tf_op jit(solution)/shard_map/dot_general | solution.py:125
  93.1 7.9 %fusion.5 = bf16[256,8192]{1,0:T(8,128)(2,1)} fusion(f32[256,8192]{1,0:T(8,128)S(1)} %fusion.6, bf16[1024,8192]{1,0:T(8,128)(2,1)} %param.18, bf16[256,1024]{1,0:T(8,128)(2,1)S(1)} %convolution_convert_fusion.4), kind=kOutput, calls=%fused_computation.11 | convolution fusion | flops 2155872256 | bytes 21233664 | tf_op jit(solution)/shard_map/dot_general | solution.py:125
  101.2 44.6 %reduce-scatter.2.cloned.1.call-done = bf16[256,2048]{1,0:T(8,128)(2,1)} async-done(((bf16[256,8192]{1,0:T(8,128)(2,1)}), bf16[256,2048]{1,0:T(8,128)(2,1)}) %reduce-scatter.2.cloned.1.call-update) | async-done | bytes 1048592 | tf_op jit(solution)/shard_map/reduce_scatter | solution.py:131
  145.8 2.1 convolution_convert_fusion.2
  147.9 36.8 %all_to_all.5 = bf16[8,40,2048]{2,1,0:T(8,128)(2,1)} all-to-all(bf16[8,40,2048]{2,1,0:T(8,128)(2,1)S(1)} %bitcast.38), channel_id=1, replica_groups=mesh['grp'=8,'tp'=4] {'grp'}, dimensions={0} | all-to-all | bytes 2621440 | tf_op jit(solution)/shard_map/all_to_all | solution.py:142
  184.7 38.6 %all-gather.5.cloned.1.call-done = bf16[320,8192]{1,0:T(8,128)(2,1)} async-done(((bf16[320,2048]{1,0:T(8,128)(2,1)}), bf16[320,8192]{1,0:T(8,128)(2,1)}) %all-gather.5.cloned.1.call-update) | async-done | bytes 5242896 | tf_op jit(solution)/shard_map/all_gather | solution.py:143
  223.3 3.8 %fusion = f32[320]{0:T(512)S(1)} fusion(bf16[320,8192]{1,0:T(8,128)(2,1)} %all-gather.5.cloned.1.call-done), kind=kLoop, calls=%fused_computation.4 | loop fusion | flops 7864000 | bytes 5244160 | tf_op jit(solution)/shard_map/reduce_sum | solution.py:18
  227.1 0.3 copy-done
  227.4 4.5 %fusion.27 = bf16[320,256]{1,0:T(8,128)(2,1)} fusion(bf16[8192,256]{1,0:T(8,128)(2,1)} %param.25, bf16[320,8192]{1,0:T(8,128)(2,1)S(1)} %copy-done, f32[8192]{0:T(1024)S(1)} %convert_element_type.111, f32[320]{0:T(512)S(1)} %add_rsqrt_fusion), kind=kOutput, calls=%fused_computation.45 | convolution fusion | flops 1352744960 | bytes 9635072 | tf_op jit(solution)/shard_map/dot_general | solution.py:146
  (37 shorter events, 0.9 us)
Async XLA Ops:
  6.5 7.5 %copy-start.3 = (bf16[16,320,256]{2,1,0:T(8,128)(2,1)S(1)}, bf16[16,320,256]{2,1,0:T(8,128)(2,1)}, u32[]{:S(2)}) copy-start(bf16[16,320,256]{2,1,0:T(8,128)(2,1)} %param.20) | copy-start | bytes 7864324
  6.5 39.6 %all-gather.3.cloned.1.call-start = ((), (), s32[]{:S(2)}) async-start(), calls=%async_computation.2 | async-start | bytes 5242880 | tf_op jit(solution)/shard_map/all_gather | solution.py:92
  7.3 138.5 %reduce-scatter.2.cloned.1.call-start = ((), (), s32[]{:S(2)}) async-start(), calls=%async_computation.3 | async-start | bytes 5242880 | tf_op jit(solution)/shard_map/reduce_scatter | solution.py:131
  9.1 7.8 %copy-start.7 = (s32[16,1]{0,1:T(1,128)S(1)}, s32[16,1]{0,1:T(1,128)}, u32[]{:S(2)}) copy-start(s32[16,1]{0,1:T(1,128)} %param.23) | copy-start | bytes 196
  9.1 8.0 %copy-start.5 = (s32[1,256]{1,0:T(1,128)S(1)}, s32[1,256]{1,0:T(1,128)}, u32[]{:S(2)}) copy-start(s32[1,256]{1,0:T(1,128)} %param.21) | copy-start | bytes 3076
  9.1 8.2 %copy-start.6 = (s32[1,16]{1,0:T(1,128)S(1)}, s32[1,16]{1,0:T(1,128)}, u32[]{:S(2)}) copy-start(s32[1,16]{1,0:T(1,128)} %param.22) | copy-start | bytes 196
  71.6 2.1 copy-start.1
  80.5 2.3 copy-start.2
  101.1 83.6 %copy-start.4 = (bf16[8192]{0:T(1024)(128)(2,1)S(1)}, bf16[8192]{0:T(1024)(128)(2,1)}, u32[]{:S(2)}) copy-start(bf16[8192]{0:T(1024)(128)(2,1)} %param.24) | copy-start | bytes 49156
  101.1 122.3 %all-gather.5.cloned.1.call-start = ((), (), s32[]{:S(2)}) async-start(), calls=%async_computation.4 | async-start | bytes 6553600 | tf_op jit(solution)/shard_map/all_gather | solution.py:143
  223.3 4.0 %copy-start = (bf16[320,8192]{1,0:T(8,128)(2,1)S(1)}, bf16[320,8192]{1,0:T(8,128)(2,1)}, u32[]{:S(2)}) copy-start(bf16[320,8192]{1,0:T(8,128)(2,1)} %all-gather.5.cloned.1.call-done) | copy-start | bytes 15728644
Sparse Core Ops, SparseCore 0:
  8.9 37.1 all-gather.2
  101.2 44.5 reduce-scatter.1
  184.8 38.5 all-gather.4
where the time goes:
time: 239 us; the launch traced here: 238 us
  waiting for transfers between devices  113 us (47%)
  matrix products  51.4 us (22%)
  blocking collectives  36.8 us (15%)
  between operations  13.3 us (6%)
  local copies, waits for them, and re-layouts  12.8 us (5%)
  other arithmetic  11.4 us (5%)
    reduce_scatter x1, waiting for transfers between devices, on_device(): lax.psum_scatter(head_total.astype(jnp.bfloat16), 'tp', scatter_dimension...  44.6 us
    all_gather x1, waiting for transfers between devices, on_device(): lax.all_gather(arrived.reshape(owner_count * CAPS * MOST, share), 'tp', a...  38.6 us
    all_to_all x1, blocking collectives, on_device(): lax.all_to_all(outgoing, 'grp', split_axis=0, concat_axis=0, tiled=True)  36.8 us
    all_gather x1, waiting for transfers between devices, on_device(): gathered = lax.all_gather(thinker_rows, 'tp', axis=0, tiled=True)  28.6 us
    dot_general x2, matrix products, on_device(): jnp.dot(attention_rows[:, lower:lower + head_width], w_out[lower:lower +...  13.6 us
    dot_general x1, matrix products, on_device(): jnp.dot(placing, query, preferred_element_type=jnp.float32)  11.8 us
    reduce_sum x2, other arithmetic, rms_scaled(): mean_square = jnp.mean(floats * floats, axis=-1, keepdims=True)  6.87 us
    dot_general x1, matrix products, on_device(): jnp.dot(placing, key_new, preferred_element_type=jnp.float32)  5 us
  transfers between devices with their start and end apart: 3, of which 3 were waited for; matrix products, arithmetic and copies ran while one was open for 4% of the time, Pallas kernels for 0%

commit v1 on v0

v1 whole, which is shorter than its diff:
```python
import functools

import jax
import jax.numpy as jnp
from jax import lax
from jax.experimental import pallas as pl
from jax.experimental.pallas import tpu as pltpu
from jax.sharding import PartitionSpec as P

HEAD_DIM = 128
SESS = 16
CAPS = 2
GQA = 4
MOST = 20
OWNER_PITCH = 48
CHUNKS = 8
VMEM_BYTES = 58 * 1024 * 1024

EPSILON = 1e-06
MESH = pl.DeviceIdType.MESH


def places(n_tp):
    me = lax.axis_index("tp")
    core = lax.rem(me, 2)
    chip = me // 2
    return me, chip, core, me + 1 - 2 * core


def greet(n_tp, n_grp=1):
    me, chip, core, sibling = places(n_tp)
    n_chips = n_tp // 2
    barrier = pltpu.get_barrier_semaphore()
    peers = [{"tp": sibling}]
    for j in range(1, n_chips):
        peers.append({"tp": lax.rem(chip + j, n_chips) * 2 + core})
    grp = lax.axis_index("grp")
    for j in range(1, n_grp):
        peers.append({"grp": lax.rem(grp + j, n_grp)})
    for peer in peers:
        pl.semaphore_signal(barrier, inc=1, device_id=peer, device_id_type=MESH)
    pl.semaphore_wait(barrier, len(peers))


def remote(src, dst, send, recv, device):
    return pltpu.make_async_remote_copy(
        src_ref=src,
        dst_ref=dst,
        send_sem=send,
        recv_sem=recv,
        device_id=device,
        device_id_type=MESH,
    )


class RowGather:
    def __init__(self, n_tp, held, sib_send, chip_send, pass_send, recv):
        self.held, self.recv = held, recv
        self.sib_send, self.chip_send, self.pass_send = sib_send, chip_send, pass_send
        self.me, self.chip, self.core, self.sibling = places(n_tp)
        self.n_chips = n_tp // 2
        self.rows = held.shape[1] // n_tp

    def block(self, f, owner):
        start = pl.multiple_of(owner * self.rows, self.rows)
        return self.held.at[f, pl.ds(start, self.rows), :]

    def copy(self, f, owner, send, target):
        ref = self.block(f, owner)
        return remote(ref, ref, send, self.recv.at[f, owner], {"tp": target})

    def partner(self, j):
        return lax.rem(self.chip + j, self.n_chips) * 2 + self.core

    def own_copies(self, f):
        copies = [
            self.copy(f, self.me, self.chip_send.at[f, j - 1], self.partner(j))
            for j in range(1, self.n_chips)
        ]
        return copies + [self.copy(f, self.me, self.sib_send.at[f], self.sibling)]

    def passed_copies(self, f):
        return [
            self.copy(f, self.partner(j), self.pass_send.at[f, j - 1], self.sibling)
            for j in range(1, self.n_chips)
        ]

    def send(self, f):
        for copy in self.own_copies(f):
            copy.start()

    def pass_on(self, f):
        for copy in self.passed_copies(f):
            copy.wait_recv()
            copy.start()

    def wait_sibling(self, f):
        self.copy(f, self.sibling, self.sib_send.at[f], self.sibling).wait_recv()
        for j in range(1, self.n_chips):
            owner = lax.rem(self.chip + j, self.n_chips) * 2 + 1 - self.core
            self.copy(f, owner, self.pass_send.at[f, j - 1], self.sibling).wait_recv()

    def wait_sends(self, f):
        for copy in self.own_copies(f) + self.passed_copies(f):
            copy.wait_send()


def gather_scratch(n_tp, rows, width):
    other = max(1, n_tp // 2 - 1)
    return [
        pltpu.VMEM((CHUNKS, n_tp * rows, width), jnp.bfloat16),
        pltpu.SemaphoreType.DMA((CHUNKS,)),
        pltpu.SemaphoreType.DMA((CHUNKS, other)),
        pltpu.SemaphoreType.DMA((CHUNKS, other)),
        pltpu.SemaphoreType.DMA((CHUNKS, n_tp)),
    ]


def column_tile(columns):
    return 512 if columns % 512 == 0 else 256 if columns % 256 == 0 else 128


def project_kernel(
    n_tp, x_ref, gain_ref, wq_ref, wk_ref, wv_ref, out_ref,
    held, sib_send, chip_send, pass_send, recv, weights, total, w_sem,
):
    width = held.shape[2]
    model_width = width * CHUNKS
    edges = [0]
    for ref in (wq_ref, wk_ref, wv_ref):
        edges.append(edges[-1] + ref.shape[1])

    def weight_copies(f):
        start = pl.multiple_of(f * width, width)
        return [
            pltpu.make_async_copy(
                ref.at[pl.ds(start, width), :],
                weights.at[f, :, pl.ds(edges[i], ref.shape[1])],
                w_sem.at[f, i],
            )
            for i, ref in enumerate((wq_ref, wk_ref, wv_ref))
        ]

    def start_weights(f, carry):
        for copy in weight_copies(f):
            copy.start()
        return carry

    lax.fori_loop(0, CHUNKS, start_weights, 0)
    greet(n_tp)
    gather = RowGather(n_tp, held, sib_send, chip_send, pass_send, recv)

    def squares(f, carry):
        part = x_ref[:, pl.ds(pl.multiple_of(f * width, width), width)].astype(jnp.float32)
        return carry + jnp.sum(part * part, axis=1, keepdims=True)

    square_sum = lax.fori_loop(
        0, CHUNKS, squares, jnp.zeros((x_ref.shape[0], 1), jnp.float32)
    )
    scale = lax.rsqrt(square_sum / model_width + EPSILON)
    rows = gather.rows

    def normalise(f, carry):
        columns = pl.ds(pl.multiple_of(f * width, width), width)
        part = x_ref[:, columns].astype(jnp.float32) * scale
        part = part * gain_ref[:, columns].astype(jnp.float32)
        start = pl.multiple_of(gather.me * rows, rows)
        held[f, pl.ds(start, rows), :] = part.astype(jnp.bfloat16)
        gather.send(f)
        return carry

    lax.fori_loop(0, CHUNKS, normalise, 0)
    total[...] = jnp.zeros_like(total)
    tile = column_tile(total.shape[1])

    def step(f, carry):
        @pl.when(f < CHUNKS)
        def _():
            gather.pass_on(f)

        @pl.when(f >= 1)
        def _():
            g = f - 1
            gather.wait_sibling(g)
            for copy in weight_copies(g):
                copy.wait()
            for lower in range(0, total.shape[1], tile):
                total[:, lower : lower + tile] += jnp.dot(
                    held[g],
                    weights[g, :, lower : lower + tile],
                    preferred_element_type=jnp.float32,
                )

        return carry

    lax.fori_loop(0, CHUNKS + 1, step, 0)
    out_ref[...] = total[...].astype(jnp.bfloat16)

    def finish(f, carry):
        gather.wait_sends(f)
        return carry

    lax.fori_loop(0, CHUNKS, finish, 0)


def project(n_tp, rows_here, gain, w_query, w_key, w_value):
    rows, model_width = rows_here.shape
    width = model_width // CHUNKS
    columns = w_query.shape[1] + w_key.shape[1] + w_value.shape[1]
    vmem, hbm = pl.BlockSpec(memory_space=pltpu.VMEM), pl.BlockSpec(memory_space=pl.ANY)
    return pl.pallas_call(
        functools.partial(project_kernel, n_tp),
        out_shape=jax.ShapeDtypeStruct((n_tp * rows, columns), jnp.bfloat16),
        in_specs=[vmem, vmem, hbm, hbm, hbm],
        out_specs=vmem,
        scratch_shapes=gather_scratch(n_tp, rows, width)
        + [
            pltpu.VMEM((CHUNKS, width, columns), jnp.bfloat16),
            pltpu.VMEM((n_tp * rows, columns), jnp.float32),
            pltpu.SemaphoreType.DMA((CHUNKS, 3)),
        ],
        compiler_params=pltpu.CompilerParams(
            collective_id=0, has_side_effects=True, vmem_limit_bytes=VMEM_BYTES
        ),
        name="gather_project",
    )(rows_here, gain.reshape(1, model_width), w_query, w_key, w_value)


def talk_kernel(
    n_tp, n_grp, attended_ref, wo_ref, x_ref, gain_ref, wt_ref, routing_ref, out_ref,
    held, sib_send, chip_send, pass_send, recv,
    ordered, w_out, w_talk, kept, pair_out, pair_in, chip_out, chip_in,
    total, square_sum, owner_out, owner_in,
    wo_sem, wt_sem, pair_send, pair_recv, part_send, part_recv, owner_send, owner_recv,
):
    width = held.shape[2]
    model_width = width * CHUNKS
    head_width = GQA * HEAD_DIM

    def weight_copies(f):
        start = pl.multiple_of(f * width, width)
        return (
            pltpu.make_async_copy(wo_ref.at[:, pl.ds(start, width)], w_out.at[f], wo_sem.at[f]),
            pltpu.make_async_copy(wt_ref.at[pl.ds(start, width), :], w_talk.at[f], wt_sem.at[f]),
        )

    def start_weights(which):
        def body(f, carry):
            weight_copies(f)[which].start()
            return carry

        lax.fori_loop(0, CHUNKS, body, 0)

    start_weights(0)
    start_weights(1)
    gather = RowGather(n_tp, held, sib_send, chip_send, pass_send, recv)
    me, chip, core, sibling = gather.me, gather.chip, gather.core, gather.sibling
    n_chips, rows = gather.n_chips, gather.rows
    half = n_chips * rows
    for c in range(n_chips):
        for side, owner in enumerate((2 * c + 1 - core, 2 * c + core)):
            ordered[side * half + c * rows : side * half + (c + 1) * rows, :] = attended_ref[
                pl.ds(pl.multiple_of(owner * rows, rows), rows), :
            ]
    greet(n_tp, n_grp)

    def pair_copy(f):
        return remote(
            pair_out.at[f], pair_in.at[f], pair_send.at[f], pair_recv.at[f], {"tp": sibling}
        )

    def part_copy(f, j):
        return remote(
            chip_out.at[f, j - 1],
            chip_in.at[f, j - 1],
            part_send.at[f, j - 1],
            part_recv.at[f, j - 1],
            {"tp": gather.partner(j)},
        )

    tile = column_tile(width)

    def reduce_step(f, carry):
        @pl.when(f < CHUNKS)
        def _():
            weight_copies(f)[0].wait()
            for lower in range(0, width, tile):
                summed = None
                for first in range(0, ordered.shape[1], head_width):
                    part = jnp.dot(
                        ordered[:, first : first + head_width],
                        w_out[f, first : first + head_width, lower : lower + tile],
                        preferred_element_type=jnp.float32,
                    )
                    part = part.astype(jnp.bfloat16).astype(jnp.float32)
                    summed = part if summed is None else summed + part
                pair_out[f, :, lower : lower + tile] = summed[:half].astype(jnp.bfloat16)
                kept[f, :, lower : lower + tile] = summed[half:]
            pair_copy(f).start()

        @pl.when(f >= 1)
        def _():
            g = f - 1
            pair_copy(g).wait_recv()
            for j in range(1, n_chips):
                there = pl.ds(pl.multiple_of(lax.rem(chip + j, n_chips) * rows, rows), rows)
                both = kept[g, there, :] + pair_in[g, there, :].astype(jnp.float32)
                chip_out[g, j - 1] = both.astype(jnp.bfloat16)
                part_copy(g, j).start()

        return carry

    lax.fori_loop(0, CHUNKS + 1, reduce_step, 0)

    def hidden_step(f, carry):
        here = pl.ds(pl.multiple_of(chip * rows, rows), rows)
        both = kept[f, here, :] + pair_in[f, here, :].astype(jnp.float32)
        for j in range(1, n_chips):
            part_copy(f, j).wait_recv()
            both = both + chip_in[f, j - 1].astype(jnp.float32)
        columns = pl.ds(pl.multiple_of(f * width, width), width)
        hidden = x_ref[:, columns].astype(jnp.float32) + both
        held[f, pl.ds(pl.multiple_of(me * rows, rows), rows), :] = hidden.astype(jnp.bfloat16)
        gather.send(f)
        return carry

    lax.fori_loop(0, CHUNKS, hidden_step, 0)
    total[...] = jnp.zeros_like(total)
    square_sum[...] = jnp.zeros_like(square_sum)

    def talk_step(f, carry):
        @pl.when(f < CHUNKS)
        def _():
            gather.pass_on(f)

        @pl.when(f >= 1)
        def _():
            g = f - 1
            gather.wait_sibling(g)
            weight_copies(g)[1].wait()
            hidden = held[g].astype(jnp.float32)
            square_sum[...] += jnp.sum(hidden * hidden, axis=1, keepdims=True)
            columns = pl.ds(pl.multiple_of(g * width, width), width)
            gained = (hidden * gain_ref[:, columns].astype(jnp.float32)).astype(jnp.bfloat16)
            total[...] += jnp.dot(gained, w_talk[g], preferred_element_type=jnp.float32)

        return carry

    lax.fori_loop(0, CHUNKS + 1, talk_step, 0)
    scale = lax.rsqrt(square_sum[...] / model_width + EPSILON)
    talk = (total[...] * scale).astype(jnp.bfloat16)
    pitch = owner_out.shape[1]
    grp = lax.axis_index("grp")

    def owner_copy(j):
        target = lax.rem(grp + j, n_grp)
        return remote(
            owner_out.at[target],
            owner_in.at[j],
            owner_send.at[j],
            owner_recv.at[j],
            {"grp": target},
        )

    routed = jnp.dot(routing_ref[...], talk, preferred_element_type=jnp.float32)
    for o in range(n_grp):
        owner_out[o] = routed[o * pitch : (o + 1) * pitch].astype(jnp.bfloat16)
    for j in range(1, n_grp):
        owner_copy(j).start()
    out_ref[grp] = owner_out[grp]
    for j in range(1, n_grp):
        owner_copy(j).wait_recv()
        out_ref[lax.rem(grp + n_grp - j, n_grp)] = owner_in[j]

    def finish(f, carry):
        gather.wait_sends(f)
        pair_copy(f).wait_send()
        for j in range(1, n_chips):
            part_copy(f, j).wait_send()
        return carry

    lax.fori_loop(0, CHUNKS, finish, 0)
    for j in range(1, n_grp):
        owner_copy(j).wait_send()


def talk(n_tp, n_grp, attended, w_out, rows_here, gain, w_talker, routing):
    rows, model_width = rows_here.shape
    width = model_width // CHUNKS
    columns = w_talker.shape[1]
    other = max(1, n_tp // 2 - 1)
    half = n_tp // 2 * rows
    pitch = routing.shape[0] // n_grp
    vmem, hbm = pl.BlockSpec(memory_space=pltpu.VMEM), pl.BlockSpec(memory_space=pl.ANY)
    bf16, dma = jnp.bfloat16, pltpu.SemaphoreType.DMA
    return pl.pallas_call(
        functools.partial(talk_kernel, n_tp, n_grp),
        out_shape=jax.ShapeDtypeStruct((n_grp, pitch, columns), bf16),
        in_specs=[vmem, hbm, vmem, vmem, hbm, vmem],
        out_specs=vmem,
        scratch_shapes=gather_scratch(n_tp, rows, width)
        + [
            pltpu.VMEM(attended.shape, bf16),
            pltpu.VMEM((CHUNKS, w_out.shape[0], width), bf16),
            pltpu.VMEM((CHUNKS, width, columns), bf16),
            pltpu.VMEM((CHUNKS, half, width), jnp.float32),
            pltpu.VMEM((CHUNKS, half, width), bf16),
            pltpu.VMEM((CHUNKS, half, width), bf16),
            pltpu.VMEM((CHUNKS, other, rows, width), bf16),
            pltpu.VMEM((CHUNKS, other, rows, width), bf16),
            pltpu.VMEM((n_tp * rows, columns), jnp.float32),
            pltpu.VMEM((n_tp * rows, 1), jnp.float32),
            pltpu.VMEM((n_grp, pitch, columns), bf16),
            pltpu.VMEM((n_grp, pitch, columns), bf16),
            dma((CHUNKS,)),
            dma((CHUNKS,)),
            dma((CHUNKS,)),
            dma((CHUNKS,)),
            dma((CHUNKS, other)),
            dma((CHUNKS, other)),
            dma((n_grp,)),
            dma((n_grp,)),
        ],
        compiler_params=pltpu.CompilerParams(
            collective_id=1, has_side_effects=True, vmem_limit_bytes=VMEM_BYTES
        ),
        name="reduce_talk",
    )(attended, w_out, rows_here, gain.reshape(1, model_width), w_talker, routing)


def slot_tables(session_row, owner_row):
    session_range = jnp.arange(SESS, dtype=jnp.int32)
    member = (session_row[:, None] == session_range[None, :]).astype(jnp.int32)
    counts = jnp.sum(member, axis=0)
    starts = jnp.cumsum(counts) - counts
    first_row = jnp.sum(member * starts[None, :], axis=1)
    position = jnp.arange(session_row.shape[0], dtype=jnp.int32) - first_row
    earlier = (owner_row[:, None] == owner_row[None, :]) & (
        session_range[None, :] < session_range[:, None]
    )
    owner_rank = jnp.sum(earlier.astype(jnp.int32), axis=1)
    owner_slot = owner_row * OWNER_PITCH + owner_rank * MOST
    destination = jnp.sum(member * owner_slot[None, :], axis=1) + position
    return (counts, position, destination)


def attend(q_slots, k_slots, v_slots, cache_k, cache_v, live_lens, counts):
    score_scale = HEAD_DIM ** (-0.5)
    cached = (
        jnp.einsum("smkgd,sckd->skgmc", q_slots, cache_k, preferred_element_type=jnp.float32)
        * score_scale
    )
    fresh = (
        jnp.einsum("smkgd,snkd->skgmn", q_slots, k_slots, preferred_element_type=jnp.float32)
        * score_scale
    )
    live_cache = jnp.arange(cache_k.shape[1], dtype=jnp.int32)[None, :] < live_lens[:, None]
    places = jnp.arange(MOST, dtype=jnp.int32)
    causal = places[None, :] <= places[:, None]
    live_fresh = causal[None, :, :] & (places[None, None, :] < counts[:, None, None])
    cached = jnp.where(live_cache[:, None, None, None, :], cached, -1e30)
    fresh = jnp.where(live_fresh[:, None, None, :, :], fresh, -1e30)
    highest = jnp.maximum(jnp.max(cached, axis=-1), jnp.max(fresh, axis=-1))
    exp_cached = jnp.exp(cached - highest[..., None])
    exp_fresh = jnp.exp(fresh - highest[..., None])
    denominator = jnp.sum(exp_cached, axis=-1) + jnp.sum(exp_fresh, axis=-1)
    weight_cached = (exp_cached / denominator[..., None]).astype(jnp.bfloat16)
    weight_fresh = (exp_fresh / denominator[..., None]).astype(jnp.bfloat16)
    mixed = jnp.einsum(
        "skgmc,sckd->smkgd", weight_cached, cache_v, preferred_element_type=jnp.float32
    )
    mixed = mixed + jnp.einsum(
        "skgmn,snkd->smkgd", weight_fresh, v_slots, preferred_element_type=jnp.float32
    )
    return mixed.astype(jnp.bfloat16)


def on_device(
    thinker_rows,
    norm_gain,
    w_query,
    w_key,
    w_value,
    w_out,
    cache_keys,
    cache_values,
    session_ids,
    cache_lens,
    owners,
    talker_gain,
    w_talker,
):
    n_tp, n_grp = lax.axis_size("tp"), lax.axis_size("grp")
    kv_local = w_key.shape[1] // HEAD_DIM
    head_width = GQA * HEAD_DIM
    slot_count = SESS * MOST
    qkv = project(n_tp, thinker_rows, norm_gain, w_query, w_key, w_value)
    counts, position, destination = slot_tables(session_ids[0], owners[:, 0])
    slot_index = session_ids[0] * MOST + position
    placing = (slot_index[None, :] == jnp.arange(slot_count, dtype=jnp.int32)[:, None]).astype(
        jnp.bfloat16
    )
    slots = jnp.dot(placing, qkv, preferred_element_type=jnp.float32).astype(jnp.bfloat16)
    q_slots, k_slots, v_slots = jnp.split(
        slots, [w_query.shape[1], w_query.shape[1] + w_key.shape[1]], axis=1
    )
    mixed = attend(
        q_slots.reshape(SESS, MOST, kv_local, GQA, HEAD_DIM),
        k_slots.reshape(SESS, MOST, kv_local, HEAD_DIM),
        v_slots.reshape(SESS, MOST, kv_local, HEAD_DIM),
        cache_keys.reshape(SESS, cache_keys.shape[1], kv_local, HEAD_DIM),
        cache_values.reshape(SESS, cache_values.shape[1], kv_local, HEAD_DIM),
        cache_lens[0],
        counts,
    )
    attended = lax.dot_general(
        placing,
        mixed.reshape(slot_count, kv_local * head_width),
        (((0,), (0,)), ((), ())),
        preferred_element_type=jnp.float32,
    ).astype(jnp.bfloat16)
    routing = (
        destination[None, :] == jnp.arange(n_grp * OWNER_PITCH, dtype=jnp.int32)[:, None]
    ).astype(jnp.bfloat16)
    placed = talk(n_tp, n_grp, attended, w_out, thinker_rows, talker_gain, w_talker, routing)
    return placed[:, : CAPS * MOST].reshape(n_grp * CAPS * MOST, w_talker.shape[1])


def solution(mesh):
    return jax.shard_map(
        on_device,
        mesh=mesh,
        in_specs=(
            P(("grp", "tp"), None),
            P(),
            P(None, "tp"),
            P(None, "tp"),
            P(None, "tp"),
            P("tp", None),
            P("grp", None, "tp"),
            P("grp", None, "tp"),
            P("grp", None),
            P("grp", None),
            P("grp", None),
            P(),
            P(None, "tp"),
        ),
        out_specs=P("grp", "tp"),
        check_vma=False,
    )
```

time: 239 us -> 130 us (0.54)
  waiting for transfers between devices: 113 us -> 0 us
  Pallas kernels: 0 us -> 95.6 us
  matrix products: 51.4 us -> 13.4 us
  blocking collectives: 36.8 us -> 0 us
  between operations: 13.3 us -> 0.16 us
  other arithmetic: 11.4 us -> 7.03 us
    pallas_call x0 -> x2, Pallas kernels: none -> 95.6 us  [the longest x1 62.9 us: talk(): pl.pallas_call(functools.partial(talk_kernel, n_tp, n_grp), out_shape=jax...]
    all_gather x2 -> x0, waiting for transfers between devices: 67.3 us -> none  [the longest x1 38.6 us: on_device(): lax.all_gather(arrived.reshape(owner_count * CAPS * MOST, share), 'tp', a...]
    reduce_scatter x1 -> x0, waiting for transfers between devices: 44.6 us -> none  [on_device(): lax.psum_scatter(head_total.astype(jnp.bfloat16), 'tp', scatter_dimension...]
    dot_general x7 -> x1, matrix products: 42.1 us -> 1.56 us  [on_device(): jnp.dot(placing, qkv, preferred_element_type=jnp.float32)]
    all_to_all x1 -> x0, blocking collectives: 36.8 us -> none  [on_device(): lax.all_to_all(outgoing, 'grp', split_axis=0, concat_axis=0, tiled=True)]
    reduce_sum x3 -> x1, other arithmetic: 6.96 us -> 0.76 us  [slot_tables(): destination = jnp.sum(member * owner_slot[None, :], axis=1) + position]
    unnamed x16 -> x6, local copies, waits for them, and re-layouts: 3.67 us -> 0.08 us
  transfers between devices with their start and end apart: 3 -> 0, of which waited for: 3 -> 0; matrix products, arithmetic and copies ran while one was open for 4% -> 0% of each run, Pallas kernels for 0% -> 0%
where the time goes in v1:
time: 130 us
  Pallas kernels  95.6 us (74%)
  local copies, waits for them, and re-layouts  13.6 us (10%)
  matrix products  13.4 us (10%)
  other arithmetic  7.03 us (5%)
    pallas_call x1, Pallas kernels, talk(): pl.pallas_call(functools.partial(talk_kernel, n_tp, n_grp), out_shape=jax...  62.9 us
    pallas_call x1, Pallas kernels, project(): pl.pallas_call(functools.partial(project_kernel, n_tp), out_shape=jax.Sha...  32.7 us
    reshape x1, local copies, waits for them, and re-layouts, on_device(): cache_keys.reshape(SESS, cache_keys.shape[1], kv_local, HEAD_DIM)  4.9 us
    dot_general x1, matrix products, attend(): jnp.einsum('skgmc,sckd->smkgd', weight_cached, cache_v, preferred_element...  3.83 us
    dot_general x1, matrix products, attend(): jnp.einsum('smkgd,sckd->skgmc', q_slots, cache_k, preferred_element_type=...  3.54 us
    reshape x1, local copies, waits for them, and re-layouts, on_device(): cache_values.reshape(SESS, cache_values.shape[1], kv_local, HEAD_DIM)  3.54 us

profile of v1, /device:TPU:0, one launch (start us, length us, event | category | flops | bytes accessed | tf_op | source)
XLA Modules:
  0.0 129.7 jit_solution(6047853775531986041)
XLA Ops:
  0.0 0.8 convert_reduce_fusion
  0.8 0.1 copy.31
  0.9 0.1 reduce
  1.0 0.9 convert_reduce_fusion.1
  2.0 0.7 multiply_add_fusion
  2.6 0.8 select_reduce_fusion
  3.4 0.7 subtract_add_fusion.1
  4.1 1.3 %reshape.151.gain_ref = bf16[1,8192]{1,0:T(2,128)(2,1)} reshape(bf16[8192]{0:T(1024)(128)(2,1)} %param.14) | data formatting | bytes 32768 | tf_op jit(solution)/shard_map/reshape | solution.py:226
  5.4 32.7 %gather_project.1 = bf16[256,1536]{1,0:T(8,128)(2,1)} custom-call(bf16[64,8192]{1,0:T(8,128)(2,1)} %x_ref.3, bf16[1,8192]{1,0:T(2,128)(2,1)} %reshape.151.gain_ref, bf16[8192,1024]{1,0:T(8,128)(2,1)} %wq_ref.1, bf16[8192,256]{1,0:T(8,128)(2,1)} %wk_ref.1, bf16[8192,256]{1,0:T(8,128)(2,1)} %wv_ref.1), custom_call_target="tpu_custom_call" | custom-call | tf_op jit(solution)/shard_map/gather_project/pallas_call | solution.py:211
  38.1 1.6 %convolution_convert_fusion = bf16[320,1536]{1,0:T(8,128)(2,1)S(1)} fusion(bf16[256,1536]{1,0:T(8,128)(2,1)} %gather_project.1, s32[256]{0:T(256)S(1)} %bitcast.39), kind=kOutput, calls=%fused_computation.6 | convolution fusion | flops 252231680 | bytes 1770496 | tf_op jit(solution)/shard_map/dot_general | solution.py:503
  39.7 0.1 split.12
  39.8 0.5 reshape.152
  40.3 0.1 iota_compare_fusion.8
  40.4 0.1 broadcast_and_fusion
  40.5 1.5 %fusion.23 = (f32[16,2,4,20]{3,2,1,0:T(4,128)S(1)}, f32[16,2,4,20,20]{3,4,2,1,0:T(8,128)S(1)}) fusion(bf16[16,20,2,4,128]{4,3,2,1,0:T(4,128)(2,1)S(1)} %reshape.152, bf16[16,20,2,128,1]{3,2,1,0,4:T(2,128)(2,1)S(1)} %bitcast.36, pred[16,20,20]{1,2,0:T(8,128)(4,1)S(1)} %broadcast_and_fusion), kind=kOutput, calls=%fused_computation.46 | convolution fusion | flops 13258240 | bytes 1040640 | tf_op jit(solution)/shard_map/smkgd,snkd->skgmn/dot_general | solution.py:454
  42.0 0.1 iota_compare_fusion.4
  42.1 4.9 %reshape.153 = bf16[16,320,2,128]{3,2,1,0:T(2,128)(2,1)} reshape(bf16[16,320,256]{2,1,0:T(8,128)(2,1)} %param.19) | data formatting | bytes 5242880 | tf_op jit(solution)/shard_map/reshape | solution.py:511
  47.0 3.5 %bitcast_reduce_fusion = (f32[16,2,4,20]{3,2,1,0:T(4,128)S(1)}, f32[16,2,20,4,320]{4,2,3,1,0:T(8,128)S(1)}) fusion(pred[16,320]{1,0:T(8,128)(4,1)S(1)} %iota_compare_fusion.4, bf16[16,320,2,128,1]{3,2,1,0,4:T(2,128)(2,1)} %bitcast.35, bf16[16,20,2,4,128]{4,3,2,1,0:T(4,128)(2,1)S(1)} %reshape.152), kind=kOutput, calls=%fused_computation.1 | convolution fusion | flops 212170240 | bytes 6568960 | tf_op jit(solution)/shard_map/smkgd,sckd->skgmc/dot_general | solution.py:450
  50.6 0.5 fusion.10
  51.1 1.5 %fusion.1 = f32[16,2,4,20]{3,2,1,0:T(4,128)S(1)} fusion(f32[16,2,20,4,320]{4,2,3,1,0:T(8,128)S(1)} %get-tuple-element.10, f32[16,2,4,20]{3,2,1,0:T(4,128)S(1)} %max.7, pred[16,320]{1,0:T(8,128)(4,1)S(1)} %iota_compare_fusion.4), kind=kLoop, calls=%fused_computation.5 | loop fusion | flops 3274240 | bytes 3302400 | tf_op jit(solution)/shard_map/reduce_sum | solution.py:466
  52.6 0.1 copy-done
  52.7 1.7 %fusion.11 = f32[16,2,128,4,20]{2,4,3,1,0:T(8,128)} fusion(f32[16,2,4,20,20]{3,4,2,1,0:T(8,128)S(1)} %get-tuple-element.12, f32[16,2,4,20]{3,2,1,0:T(4,128)S(1)} %add.29, f32[16,2,4,20]{3,2,1,0:T(4,128)S(1)} %max.7, bf16[16,20,2,128,1]{3,2,1,0,4:T(2,128)(2,1)S(1)} %bitcast.37), kind=kOutput, calls=%fused_computation.19 | convolution fusion | flops 13260800 | bytes 1699840 | tf_op jit(solution)/shard_map/skgmn,snkd->smkgd/dot_general | solution.py:472
  54.4 3.5 %reshape.155 = bf16[16,320,2,128]{3,2,1,0:T(2,128)(2,1)S(1)} reshape(bf16[16,320,256]{2,1,0:T(8,128)(2,1)} %param.20) | data formatting | bytes 5242880 | tf_op jit(solution)/shard_map/reshape | solution.py:512
  58.0 3.8 %fusion.7 = bf16[16,20,2,4,128]{4,1,3,2,0:T(8,128)(2,1)S(1)} fusion(f32[16,2,128,4,20]{2,4,3,1,0:T(8,128)} %fusion.11, bf16[16,320,2,128,1]{3,2,1,0,4:T(2,128)(2,1)S(1)} %bitcast.34, f32[16,2,20,4,320]{4,2,3,1,0:T(8,128)} %copy-done, f32[16,2,4,20]{3,2,1,0:T(4,128)S(1)} %add.29, f32[16,2,4,20]{3,2,1,0:T(4,128)S(1)} %max.7, ...), kind=kOutput, calls=%fused_computation.13 | convolution fusion | flops 214466560 | bytes 7889920 | tf_op jit(solution)/shard_map/skgmc,sckd->smkgd/dot_general | solution.py:469
  61.8 0.0 copy-start.1
  61.8 0.3 copy.39
  62.1 0.5 reshape.157
  62.5 1.3 convolution_convert_fusion.1.attended_ref
  63.8 0.7 fusion.14.routing_ref
  64.6 0.6 reshape.158.gain_ref
  65.2 62.9 %reduce_talk.1 = bf16[8,48,256]{2,1,0:T(8,128)(2,1)} custom-call(bf16[256,1024]{1,0:T(8,128)(2,1)} %convolution_convert_fusion.1.attended_ref, bf16[1024,8192]{1,0:T(8,128)(2,1)} %wo_ref.1, bf16[64,8192]{1,0:T(8,128)(2,1)} %x_ref.3, bf16[1,8192]{1,0:T(2,128)(2,1)} %reshape.158.gain_ref, bf16[8192,256]{1,0:T(8,128)(2,1)} %wt_ref.1, ...), custom_call_target="tpu_custom_call" | custom-call | tf_op jit(solution)/shard_map/reduce_talk/pallas_call | solution.py:396
  128.1 1.6 %slice.3 = bf16[8,40,256]{2,1,0:T(8,128)(2,1)} slice(bf16[8,48,256]{2,1,0:T(8,128)(2,1)} %reduce_talk.1), slice={[0:8], [0:40], [0:256]} | slice | bytes 327680 | tf_op jit(solution)/shard_map/slice | solution.py:526
  (13 shorter events, 0.2 us)
Async XLA Ops:
  39.8 2.2 %copy-start.2 = (s32[1,16]{1,0:T(1,128)S(1)}, s32[1,16]{1,0:T(1,128)}, u32[]{:S(2)}) copy-start(s32[1,16]{1,0:T(1,128)} %param.22) | copy-start | bytes 196
  50.5 2.1 %copy-start = (f32[16,2,20,4,320]{4,2,3,1,0:T(8,128)}, f32[16,2,20,4,320]{4,2,3,1,0:T(8,128)S(1)}, u32[]{:S(2)}) copy-start(f32[16,2,20,4,320]{4,2,3,1,0:T(8,128)S(1)} %get-tuple-element.10) | copy-start | bytes 9830404
  61.8 2.8 %copy-start.1 = (bf16[8192]{0:T(1024)(128)(2,1)S(1)}, bf16[8192]{0:T(1024)(128)(2,1)}, u32[]{:S(2)}) copy-start(bf16[8192]{0:T(1024)(128)(2,1)} %param.24) | copy-start | bytes 49156

commit v2 on v1

--- a/solution.py
+++ b/solution.py
@@ -13,6 +13,7 @@
 GQA = 4
 MOST = 20
 OWNER_PITCH = 48
+SLOT_PITCH = 24
 CHUNKS = 8
 VMEM_BYTES = 58 * 1024 * 1024
 
@@ -39,7 +40,7 @@
         peers.append({"grp": lax.rem(grp + j, n_grp)})
     for peer in peers:
         pl.semaphore_signal(barrier, inc=1, device_id=peer, device_id_type=MESH)
-    pl.semaphore_wait(barrier, len(peers))
+    return functools.partial(pl.semaphore_wait, barrier, len(peers))
 
 
 def remote(src, dst, send, recv, device):
@@ -146,8 +147,8 @@
             copy.start()
         return carry
 
+    greeted = greet(n_tp)
     lax.fori_loop(0, CHUNKS, start_weights, 0)
-    greet(n_tp)
     gather = RowGather(n_tp, held, sib_send, chip_send, pass_send, recv)
 
     def squares(f, carry):
@@ -159,11 +160,12 @@
     )
     scale = lax.rsqrt(square_sum / model_width + EPSILON)
     rows = gather.rows
+    greeted()
 
     def normalise(f, carry):
         columns = pl.ds(pl.multiple_of(f * width, width), width)
         part = x_ref[:, columns].astype(jnp.float32) * scale
-        part = part * gain_ref[:, columns].astype(jnp.float32)
+        part = part * gain_ref[columns][None, :].astype(jnp.float32)
         start = pl.multiple_of(gather.me * rows, rows)
         held[f, pl.ds(start, rows), :] = part.astype(jnp.bfloat16)
         gather.send(f)
@@ -223,15 +225,118 @@
             collective_id=0, has_side_effects=True, vmem_limit_bytes=VMEM_BYTES
         ),
         name="gather_project",
-    )(rows_here, gain.reshape(1, model_width), w_query, w_key, w_value)
+    )(rows_here, gain, w_query, w_key, w_value)
+
+
+def slot_tables(ids_ref, owners_ref):
+    ids = ids_ref[...]
+    tokens = ids.shape[1]
+    session = lax.broadcasted_iota(jnp.int32, (SESS, tokens), 0)
+    member = (ids == session).astype(jnp.int32)
+    starts = jnp.sum((ids < session).astype(jnp.int32), axis=1, keepdims=True)
+    first = jnp.sum(member * starts, axis=0, keepdims=True)
+    position = lax.broadcasted_iota(jnp.int32, (1, tokens), 1) - first
+    one = lax.broadcasted_iota(jnp.int32, (SESS, SESS), 0)
+    two = lax.broadcasted_iota(jnp.int32, (SESS, SESS), 1)
+    named = owners_ref[...]
+    owner = jnp.sum(jnp.where(one == two, named, 0), axis=1, keepdims=True)
+    earlier = (owner == named) & (two < one)
+    rank = jnp.sum(earlier.astype(jnp.int32), axis=1, keepdims=True)
+    owner_slot = owner * OWNER_PITCH + rank * MOST
+    destination = jnp.sum(member * owner_slot, axis=0, keepdims=True) + position
+    return ids * SLOT_PITCH + position, destination
+
+
+def attend(slot, qkv_ref, cache_copies, keys, values, lens_ref, slots, mixed, attended_ref):
+    score_scale = HEAD_DIM ** (-0.5)
+    n_cache = keys.shape[1]
+    kv_local = keys.shape[2] // HEAD_DIM
+    q_width = kv_local * GQA * HEAD_DIM
+    kv_width = kv_local * HEAD_DIM
+    slot_count = SESS * SLOT_PITCH
+    slot_rows = lax.broadcasted_iota(jnp.int32, (slot_count, slot.shape[1]), 0)
+    placing = (slot_rows == slot).astype(jnp.float32)
+    tile = column_tile(slots.shape[1])
+    for lower in range(0, slots.shape[1], tile):
+        slots[:, lower : lower + tile] = jnp.dot(
+            placing.astype(jnp.bfloat16),
+            qkv_ref[:, lower : lower + tile],
+            preferred_element_type=jnp.float32,
+        )
+    many = GQA * SLOT_PITCH
+    cache_place = lax.broadcasted_iota(jnp.int32, (many, n_cache), 1)
+    row = lax.broadcasted_iota(jnp.int32, (GQA, SLOT_PITCH, SLOT_PITCH), 1)
+    column = lax.broadcasted_iota(jnp.int32, (GQA, SLOT_PITCH, SLOT_PITCH), 2)
+    row, column = row.reshape(many, SLOT_PITCH), column.reshape(many, SLOT_PITCH)
+    transposed = (((1,), (1,)), ((), ()))
+
+    def one_session(s):
+        for copy in cache_copies(s):
+            copy.wait()
+        rows = pl.ds(pl.multiple_of(s * SLOT_PITCH, 8), SLOT_PITCH)
+        live = cache_place < lens_ref[0, s]
+        for k in range(kv_local):
+            heads = [
+                slots[rows, pl.ds((k * GQA + g) * HEAD_DIM, HEAD_DIM)] for g in range(GQA)
+            ]
+            query = jnp.concatenate(heads, axis=0).astype(jnp.bfloat16)
+            lower = q_width + k * HEAD_DIM
+            key_new = slots[rows, pl.ds(lower, HEAD_DIM)].astype(jnp.bfloat16)
+            value_new = slots[rows, pl.ds(lower + kv_width, HEAD_DIM)].astype(jnp.bfloat16)
+            here = pl.ds(k * HEAD_DIM, HEAD_DIM)
+            cached = lax.dot_general(
+                query, keys[s, :, here], transposed, preferred_element_type=jnp.float32
+            )
+            fresh = lax.dot_general(
+                query, key_new, transposed, preferred_element_type=jnp.float32
+            )
+            cached = jnp.where(live, cached * score_scale, -1e30)
+            fresh = jnp.where(column <= row, fresh * score_scale, -1e30)
+            highest = jnp.maximum(
+                jnp.max(cached, axis=1, keepdims=True), jnp.max(fresh, axis=1, keepdims=True)
+            )
+            cached = jnp.exp(cached - highest)
+            fresh = jnp.exp(fresh - highest)
+            inverse = 1.0 / (
+                jnp.sum(cached, axis=1, keepdims=True) + jnp.sum(fresh, axis=1, keepdims=True)
+            )
+            sums = jnp.dot(
+                (cached * inverse).astype(jnp.bfloat16),
+                values[s, :, here],
+                preferred_element_type=jnp.float32,
+            ) + jnp.dot(
+                (fresh * inverse).astype(jnp.bfloat16),
+                value_new,
+                preferred_element_type=jnp.float32,
+            )
+            for g in range(GQA):
+                mixed[rows, pl.ds((k * GQA + g) * HEAD_DIM, HEAD_DIM)] = sums[
+                    g * SLOT_PITCH : (g + 1) * SLOT_PITCH
+                ]
+
+    def sessions(i, carry):
+        one_session(2 * i)
+        one_session(2 * i + 1)
+        return carry
+
+    lax.fori_loop(0, SESS // 2, sessions, 0)
+    back = placing.T.astype(jnp.bfloat16)
+    tile = column_tile(q_width)
+    for lower in range(0, q_width, tile):
+        attended_ref[:, lower : lower + tile] = jnp.dot(
+            back,
+            mixed[:, lower : lower + tile].astype(jnp.bfloat16),
+            preferred_element_type=jnp.float32,
+        ).astype(jnp.bfloat16)
 
 
 def talk_kernel(
-    n_tp, n_grp, attended_ref, wo_ref, x_ref, gain_ref, wt_ref, routing_ref, out_ref,
+    n_tp, n_grp, qkv_ref, ck_ref, cv_ref, ids_ref, lens_ref, owners_ref,
+    wo_ref, x_ref, gain_ref, wt_ref, out_ref,
     held, sib_send, chip_send, pass_send, recv,
     ordered, w_out, w_talk, kept, pair_out, pair_in, chip_out, chip_in,
     total, square_sum, owner_out, owner_in,
-    wo_sem, wt_sem, pair_send, pair_recv, part_send, part_recv, owner_send, owner_recv,
+    keys, values, slots, mixed, attended_ref, cache_sem, wo_sem, wt_sem, pair_send, pair_recv, part_send, part_recv, owner_send, owner_recv,
 ):
     width = held.shape[2]
     model_width = width * CHUNKS
@@ -251,8 +356,23 @@
 
         lax.fori_loop(0, CHUNKS, body, 0)
 
+    def cache_copies(s):
+        return (
+            pltpu.make_async_copy(ck_ref.at[s], keys.at[s], cache_sem.at[s, 0]),
+            pltpu.make_async_copy(cv_ref.at[s], values.at[s], cache_sem.at[s, 1]),
+        )
+
+    def start_cache(s, carry):
+        for copy in cache_copies(s):
+            copy.start()
+        return carry
+
+    greeted = greet(n_tp, n_grp)
+    lax.fori_loop(0, SESS, start_cache, 0)
     start_weights(0)
     start_weights(1)
+    slot, destination = slot_tables(ids_ref, owners_ref)
+    attend(slot, qkv_ref, cache_copies, keys, values, lens_ref, slots, mixed, attended_ref)
     gather = RowGather(n_tp, held, sib_send, chip_send, pass_send, recv)
     me, chip, core, sibling = gather.me, gather.chip, gather.core, gather.sibling
     n_chips, rows = gather.n_chips, gather.rows
@@ -262,7 +382,7 @@
             ordered[side * half + c * rows : side * half + (c + 1) * rows, :] = attended_ref[
                 pl.ds(pl.multiple_of(owner * rows, rows), rows), :
             ]
-    greet(n_tp, n_grp)
+    greeted()
 
     def pair_copy(f):
         return remote(
@@ -341,7 +461,7 @@
             hidden = held[g].astype(jnp.float32)
             square_sum[...] += jnp.sum(hidden * hidden, axis=1, keepdims=True)
             columns = pl.ds(pl.multiple_of(g * width, width), width)
-            gained = (hidden * gain_ref[:, columns].astype(jnp.float32)).astype(jnp.bfloat16)
+            gained = (hidden * gain_ref[columns][None, :].astype(jnp.float32)).astype(jnp.bfloat16)
             total[...] += jnp.dot(gained, w_talk[g], preferred_element_type=jnp.float32)
 
         return carry
@@ -356,21 +476,36 @@
         target = lax.rem(grp + j, n_grp)
         return remote(
             owner_out.at[target],
-            owner_in.at[j],
+            owner_in.at[grp],
             owner_send.at[j],
-            owner_recv.at[j],
+            owner_recv.at[grp],
             {"grp": target},
         )
 
-    routed = jnp.dot(routing_ref[...], talk, preferred_element_type=jnp.float32)
+    def owner_arrival(j):
+        source = lax.rem(grp + n_grp - j, n_grp)
+        return remote(
+            owner_out.at[source],
+            owner_in.at[source],
+            owner_send.at[j],
+            owner_recv.at[source],
+            {"grp": source},
+        )
+
+    routing_rows = lax.broadcasted_iota(jnp.int32, (n_grp * pitch, talk.shape[0]), 0)
+    routing = (routing_rows == destination).astype(jnp.float32).astype(jnp.bfloat16)
+    routed = jnp.dot(routing, talk, preferred_element_type=jnp.float32)
     for o in range(n_grp):
         owner_out[o] = routed[o * pitch : (o + 1) * pitch].astype(jnp.bfloat16)
     for j in range(1, n_grp):
         owner_copy(j).start()
-    out_ref[grp] = owner_out[grp]
+    owner_in[grp] = owner_out[grp]
     for j in range(1, n_grp):
-        owner_copy(j).wait_recv()
-        out_ref[lax.rem(grp + n_grp - j, n_grp)] = owner_in[j]
+        owner_arrival(j).wait_recv()
+    used = CAPS * MOST
+    out_ref[...] = jnp.concatenate(
+        [owner_in[o].astype(jnp.float32)[:used] for o in range(n_grp)], axis=0
+    ).astype(jnp.bfloat16)
 
     def finish(f, carry):
         gather.wait_sends(f)
@@ -384,23 +519,29 @@
         owner_copy(j).wait_send()
 
 
-def talk(n_tp, n_grp, attended, w_out, rows_here, gain, w_talker, routing):
+def talk(
+    n_tp, n_grp, qkv, cache_keys, cache_values, session_ids, cache_lens, owners,
+    w_out, rows_here, gain, w_talker,
+):
     rows, model_width = rows_here.shape
     width = model_width // CHUNKS
     columns = w_talker.shape[1]
     other = max(1, n_tp // 2 - 1)
     half = n_tp // 2 * rows
-    pitch = routing.shape[0] // n_grp
+    pitch = OWNER_PITCH
+    slot_count = SESS * SLOT_PITCH
+    q_width = w_out.shape[0]
     vmem, hbm = pl.BlockSpec(memory_space=pltpu.VMEM), pl.BlockSpec(memory_space=pl.ANY)
+    smem = pl.BlockSpec(memory_space=pltpu.SMEM)
     bf16, dma = jnp.bfloat16, pltpu.SemaphoreType.DMA
     return pl.pallas_call(
         functools.partial(talk_kernel, n_tp, n_grp),
-        out_shape=jax.ShapeDtypeStruct((n_grp, pitch, columns), bf16),
-        in_specs=[vmem, hbm, vmem, vmem, hbm, vmem],
+        out_shape=jax.ShapeDtypeStruct((n_grp * CAPS * MOST, columns), bf16),
+        in_specs=[vmem, hbm, hbm, vmem, smem, vmem, hbm, vmem, vmem, hbm],
         out_specs=vmem,
         scratch_shapes=gather_scratch(n_tp, rows, width)
         + [
-            pltpu.VMEM(attended.shape, bf16),
+            pltpu.VMEM((n_tp * rows, q_width), bf16),
             pltpu.VMEM((CHUNKS, w_out.shape[0], width), bf16),
             pltpu.VMEM((CHUNKS, width, columns), bf16),
             pltpu.VMEM((CHUNKS, half, width), jnp.float32),
@@ -412,6 +553,12 @@
             pltpu.VMEM((n_tp * rows, 1), jnp.float32),
             pltpu.VMEM((n_grp, pitch, columns), bf16),
             pltpu.VMEM((n_grp, pitch, columns), bf16),
+            pltpu.VMEM(cache_keys.shape, bf16),
+            pltpu.VMEM(cache_values.shape, bf16),
+            pltpu.VMEM((slot_count, qkv.shape[1]), jnp.float32),
+            pltpu.VMEM((slot_count, q_width), jnp.float32),
+            pltpu.VMEM((n_tp * rows, q_width), bf16),
+            dma((SESS, 2)),
             dma((CHUNKS,)),
             dma((CHUNKS,)),
             dma((CHUNKS,)),
@@ -424,55 +571,11 @@
         compiler_params=pltpu.CompilerParams(
             collective_id=1, has_side_effects=True, vmem_limit_bytes=VMEM_BYTES
         ),
-        name="reduce_talk",
-    )(attended, w_out, rows_here, gain.reshape(1, model_width), w_talker, routing)
-
-
-def slot_tables(session_row, owner_row):
-    session_range = jnp.arange(SESS, dtype=jnp.int32)
-    member = (session_row[:, None] == session_range[None, :]).astype(jnp.int32)
-    counts = jnp.sum(member, axis=0)
-    starts = jnp.cumsum(counts) - counts
-    first_row = jnp.sum(member * starts[None, :], axis=1)
-    position = jnp.arange(session_row.shape[0], dtype=jnp.int32) - first_row
-    earlier = (owner_row[:, None] == owner_row[None, :]) & (
-        session_range[None, :] < session_range[:, None]
+        name="attend_talk",
+    )(
+        qkv, cache_keys, cache_values, session_ids, cache_lens, owners.reshape(1, SESS),
+        w_out, rows_here, gain, w_talker,
     )
-    owner_rank = jnp.sum(earlier.astype(jnp.int32), axis=1)
-    owner_slot = owner_row * OWNER_PITCH + owner_rank * MOST
-    destination = jnp.sum(member * owner_slot[None, :], axis=1) + position
-    return (counts, position, destination)
-
-
-def attend(q_slots, k_slots, v_slots, cache_k, cache_v, live_lens, counts):
-    score_scale = HEAD_DIM ** (-0.5)
-    cached = (
-        jnp.einsum("smkgd,sckd->skgmc", q_slots, cache_k, preferred_element_type=jnp.float32)
-        * score_scale
-    )
-    fresh = (
-        jnp.einsum("smkgd,snkd->skgmn", q_slots, k_slots, preferred_element_type=jnp.float32)
-        * score_scale
-    )
-    live_cache = jnp.arange(cache_k.shape[1], dtype=jnp.int32)[None, :] < live_lens[:, None]
-    places = jnp.arange(MOST, dtype=jnp.int32)
-    causal = places[None, :] <= places[:, None]
-    live_fresh = causal[None, :, :] & (places[None, None, :] < counts[:, None, None])
-    cached = jnp.where(live_cache[:, None, None, None, :], cached, -1e30)
-    fresh = jnp.where(live_fresh[:, None, None, :, :], fresh, -1e30)
-    highest = jnp.maximum(jnp.max(cached, axis=-1), jnp.max(fresh, axis=-1))
-    exp_cached = jnp.exp(cached - highest[..., None])
-    exp_fresh = jnp.exp(fresh - highest[..., None])
-    denominator = jnp.sum(exp_cached, axis=-1) + jnp.sum(exp_fresh, axis=-1)
-    weight_cached = (exp_cached / denominator[..., None]).astype(jnp.bfloat16)
-    weight_fresh = (exp_fresh / denominator[..., None]).astype(jnp.bfloat16)
-    mixed = jnp.einsum(
-        "skgmc,sckd->smkgd", weight_cached, cache_v, preferred_element_type=jnp.float32
-    )
-    mixed = mixed + jnp.einsum(
-        "skgmn,snkd->smkgd", weight_fresh, v_slots, preferred_element_type=jnp.float32
-    )
-    return mixed.astype(jnp.bfloat16)
 
 
 def on_device(
@@ -491,39 +594,11 @@
     w_talker,
 ):
     n_tp, n_grp = lax.axis_size("tp"), lax.axis_size("grp")
-    kv_local = w_key.shape[1] // HEAD_DIM
-    head_width = GQA * HEAD_DIM
-    slot_count = SESS * MOST
     qkv = project(n_tp, thinker_rows, norm_gain, w_query, w_key, w_value)
-    counts, position, destination = slot_tables(session_ids[0], owners[:, 0])
-    slot_index = session_ids[0] * MOST + position
-    placing = (slot_index[None, :] == jnp.arange(slot_count, dtype=jnp.int32)[:, None]).astype(
-        jnp.bfloat16
+    return talk(
+        n_tp, n_grp, qkv, cache_keys, cache_values, session_ids, cache_lens, owners,
+        w_out, thinker_rows, talker_gain, w_talker,
     )
-    slots = jnp.dot(placing, qkv, preferred_element_type=jnp.float32).astype(jnp.bfloat16)
-    q_slots, k_slots, v_slots = jnp.split(
-        slots, [w_query.shape[1], w_query.shape[1] + w_key.shape[1]], axis=1
-    )
-    mixed = attend(
-        q_slots.reshape(SESS, MOST, kv_local, GQA, HEAD_DIM),
-        k_slots.reshape(SESS, MOST, kv_local, HEAD_DIM),
-        v_slots.reshape(SESS, MOST, kv_local, HEAD_DIM),
-        cache_keys.reshape(SESS, cache_keys.shape[1], kv_local, HEAD_DIM),
-        cache_values.reshape(SESS, cache_values.shape[1], kv_local, HEAD_DIM),
-        cache_lens[0],
-        counts,
-    )
-    attended = lax.dot_general(
-        placing,
-        mixed.reshape(slot_count, kv_local * head_width),
-        (((0,), (0,)), ((), ())),
-        preferred_element_type=jnp.float32,
-    ).astype(jnp.bfloat16)
-    routing = (
-        destination[None, :] == jnp.arange(n_grp * OWNER_PITCH, dtype=jnp.int32)[:, None]
-    ).astype(jnp.bfloat16)
-    placed = talk(n_tp, n_grp, attended, w_out, thinker_rows, talker_gain, w_talker, routing)
-    return placed[:, : CAPS * MOST].reshape(n_grp * CAPS * MOST, w_talker.shape[1])
 
 
 def solution(mesh):

time: 130 us -> 109 us (0.84)
  matrix products: 13.4 us -> 0 us
  Pallas kernels: 95.6 us -> 108 us
  local copies, waits for them, and re-layouts: 13.6 us -> 1.59 us
  other arithmetic: 7.03 us -> 0 us
    dot_general x6 -> x0, matrix products: 13.4 us -> none  [the longest x1 3.83 us: attend(): jnp.einsum('skgmc,sckd->smkgd', weight_cached, cache_v, preferred_element...]
    pallas_call x1, Pallas kernels: 62.9 us -> 75.6 us  [talk(): pl.pallas_call(functools.partial(talk_kernel, n_tp, n_grp), out_shape=jax...]
    reshape x8 -> x0, local copies, waits for them, and re-layouts: 11.4 us -> none  [the longest x1 4.9 us: on_device(): cache_keys.reshape(SESS, cache_keys.shape[1], kv_local, HEAD_DIM)]
    reduce_sum x5 -> x0, other arithmetic: 4.48 us -> none  [the longest x2 2.01 us: attend(): denominator = jnp.sum(exp_cached, axis=-1) + jnp.sum(exp_fresh, axis=-1)]
    slice x1 -> x0, local copies, waits for them, and re-layouts: 1.6 us -> none  [on_device(): placed[:, :CAPS * MOST].reshape(n_grp * CAPS * MOST, w_talker.shape[1])]
    unnamed x6 -> x1, local copies, waits for them, and re-layouts: 0.08 us -> 1.59 us
    add x4 -> x0, other arithmetic: 1.37 us -> none  [the longest x1 0.68 us: on_device(): slot_index = session_ids[0] * MOST + position]
where the time goes in v2:
time: 109 us
  Pallas kernels  108 us (99%)
  local copies, waits for them, and re-layouts  1.59 us (1%)
    pallas_call x1, Pallas kernels, talk(): pl.pallas_call(functools.partial(talk_kernel, n_tp, n_grp), out_shape=jax...  75.6 us
    pallas_call x1, Pallas kernels, project(): pl.pallas_call(functools.partial(project_kernel, n_tp), out_shape=jax.Sha...  32 us

profile of v2, /device:TPU:0, one launch (start us, length us, event | category | flops | bytes accessed | tf_op | source)
XLA Modules:
  0.0 109.3 jit_solution(10754562680314869660)
XLA Ops:
  0.0 32.0 %gather_project.1.qkv_ref = bf16[256,1536]{1,0:T(8,128)(2,1)} custom-call(bf16[64,8192]{1,0:T(8,128)(2,1)} %x_ref.3, bf16[8192]{0:T(1024)(128)(2,1)} %gain_ref.2, bf16[8192,1024]{1,0:T(8,128)(2,1)} %wq_ref.1, bf16[8192,256]{1,0:T(8,128)(2,1)} %wk_ref.1, bf16[8192,256]{1,0:T(8,128)(2,1)} %wv_ref.1), custom_call_target="tpu_custom_call" | custom-call | tf_op jit(solution)/shard_map/gather_project/pallas_call | solution.py:213
  32.0 75.6 %attend_talk.1 = bf16[320,256]{1,0:T(8,128)(2,1)} custom-call(bf16[256,1536]{1,0:T(8,128)(2,1)} %gather_project.1.qkv_ref, bf16[16,320,256]{2,1,0:T(8,128)(2,1)} %ck_ref.1, bf16[16,320,256]{2,1,0:T(8,128)(2,1)} %cv_ref.1, s32[1,256]{1,0:T(1,128)} %ids_ref.1, s32[1,16]{1,0:T(1,128)} %lens_ref.1, s32[1,16]{1,0:T(1,128)} %bitcast.1, bf16[1024,8192]{1,0:T(8,128)(2,1)} %wo_ref.1, ...), custom_call_target="tpu_custom_call" | custom-call | tf_op jit(solution)/shard_map/attend_talk/pallas_call | solution.py:537
  107.7 1.6 %copy.15 = bf16[320,256]{1,0:T(8,128)(2,1)} copy(bf16[320,256]{1,0:T(8,128)(2,1)} %attend_talk.1) | data formatting | bytes 327680

commit v3 on v2

--- a/solution.py
+++ b/solution.py
@@ -270,56 +270,73 @@
     row, column = row.reshape(many, SLOT_PITCH), column.reshape(many, SLOT_PITCH)
     transposed = (((1,), (1,)), ((), ()))
 
-    def one_session(s):
-        for copy in cache_copies(s):
-            copy.wait()
+    def scores(s, k):
         rows = pl.ds(pl.multiple_of(s * SLOT_PITCH, 8), SLOT_PITCH)
-        live = cache_place < lens_ref[0, s]
-        for k in range(kv_local):
-            heads = [
-                slots[rows, pl.ds((k * GQA + g) * HEAD_DIM, HEAD_DIM)] for g in range(GQA)
+        heads = [slots[rows, pl.ds((k * GQA + g) * HEAD_DIM, HEAD_DIM)] for g in range(GQA)]
+        query = jnp.concatenate(heads, axis=0).astype(jnp.bfloat16)
+        key_new = slots[rows, pl.ds(q_width + k * HEAD_DIM, HEAD_DIM)].astype(jnp.bfloat16)
+        cached = lax.dot_general(
+            query,
+            keys[s, :, pl.ds(k * HEAD_DIM, HEAD_DIM)],
+            transposed,
+            preferred_element_type=jnp.float32,
+        )
+        fresh = lax.dot_general(query, key_new, transposed, preferred_element_type=jnp.float32)
+        return cached, fresh
+
+    def masked(s, both):
+        cached = jnp.where(cache_place < lens_ref[0, s], both[0] * score_scale, -1e30)
+        return cached, jnp.where(column <= row, both[1] * score_scale, -1e30)
+
+    def peak(both):
+        return jnp.maximum(
+            jnp.max(both[0], axis=1, keepdims=True), jnp.max(both[1], axis=1, keepdims=True)
+        )
+
+    def inverse_sum(both):
+        return 1.0 / (
+            jnp.sum(both[0], axis=1, keepdims=True) + jnp.sum(both[1], axis=1, keepdims=True)
+        )
+
+    def mix(s, k, weights):
+        rows = pl.ds(pl.multiple_of(s * SLOT_PITCH, 8), SLOT_PITCH)
+        lower = q_width + kv_width + k * HEAD_DIM
+        value_new = slots[rows, pl.ds(lower, HEAD_DIM)].astype(jnp.bfloat16)
+        sums = jnp.dot(
+            weights[0],
+            values[s, :, pl.ds(k * HEAD_DIM, HEAD_DIM)],
+            preferred_element_type=jnp.float32,
+        ) + jnp.dot(weights[1], value_new, preferred_element_type=jnp.float32)
+        for g in range(GQA):
+            mixed[rows, pl.ds((k * GQA + g) * HEAD_DIM, HEAD_DIM)] = sums[
+                g * SLOT_PITCH : (g + 1) * SLOT_PITCH
             ]
-            query = jnp.concatenate(heads, axis=0).astype(jnp.bfloat16)
-            lower = q_width + k * HEAD_DIM
-            key_new = slots[rows, pl.ds(lower, HEAD_DIM)].astype(jnp.bfloat16)
-            value_new = slots[rows, pl.ds(lower + kv_width, HEAD_DIM)].astype(jnp.bfloat16)
-            here = pl.ds(k * HEAD_DIM, HEAD_DIM)
-            cached = lax.dot_general(
-                query, keys[s, :, here], transposed, preferred_element_type=jnp.float32
-            )
-            fresh = lax.dot_general(
-                query, key_new, transposed, preferred_element_type=jnp.float32
-            )
-            cached = jnp.where(live, cached * score_scale, -1e30)
-            fresh = jnp.where(column <= row, fresh * score_scale, -1e30)
-            highest = jnp.maximum(
-                jnp.max(cached, axis=1, keepdims=True), jnp.max(fresh, axis=1, keepdims=True)
-            )
-            cached = jnp.exp(cached - highest)
-            fresh = jnp.exp(fresh - highest)
-            inverse = 1.0 / (
-                jnp.sum(cached, axis=1, keepdims=True) + jnp.sum(fresh, axis=1, keepdims=True)
-            )
-            sums = jnp.dot(
-                (cached * inverse).astype(jnp.bfloat16),
-                values[s, :, here],
-                preferred_element_type=jnp.float32,
-            ) + jnp.dot(
-                (fresh * inverse).astype(jnp.bfloat16),
-                value_new,
-                preferred_element_type=jnp.float32,
-            )
-            for g in range(GQA):
-                mixed[rows, pl.ds((k * GQA + g) * HEAD_DIM, HEAD_DIM)] = sums[
-                    g * SLOT_PITCH : (g + 1) * SLOT_PITCH
-                ]
+
+    together = 4
 
     def sessions(i, carry):
-        one_session(2 * i)
-        one_session(2 * i + 1)
-        return carry
-
-    lax.fori_loop(0, SESS // 2, sessions, 0)
+        pairs = []
+        for n in range(together):
+            for copy in cache_copies(together * i + n):
+                copy.wait()
+            pairs.extend((together * i + n, k) for k in range(kv_local))
+        dots = [scores(s, k) for s, k in pairs]
+        dots = [masked(s, both) for (s, _), both in zip(pairs, dots)]
+        peaks = [peak(both) for both in dots]
+        powers = [
+            (jnp.exp(cached - highest), jnp.exp(fresh - highest))
+            for (cached, fresh), highest in zip(dots, peaks)
+        ]
+        inverses = [inverse_sum(both) for both in powers]
+        weights = [
+            ((cached * inverse).astype(jnp.bfloat16), (fresh * inverse).astype(jnp.bfloat16))
+            for (cached, fresh), inverse in zip(powers, inverses)
+        ]
+        for (s, k), both in zip(pairs, weights):
+            mix(s, k, both)
+        return carry
+
+    lax.fori_loop(0, SESS // together, sessions, 0)
     back = placing.T.astype(jnp.bfloat16)
     tile = column_tile(q_width)
     for lower in range(0, q_width, tile):

time: 109 us -> 99.9 us (0.917)
  Pallas kernels: 108 us -> 98.1 us
    pallas_call x1, Pallas kernels: 75.6 us -> 66.1 us  [talk(): pl.pallas_call(functools.partial(talk_kernel, n_tp, n_grp), out_shape=jax...]
where the time goes in v3:
time: 99.9 us; the launch traced here: 99.7 us
  Pallas kernels  98.1 us (98%)
  local copies, waits for them, and re-layouts  1.59 us (2%)
    pallas_call x1, Pallas kernels, talk(): pl.pallas_call(functools.partial(talk_kernel, n_tp, n_grp), out_shape=jax...  66.1 us
    pallas_call x1, Pallas kernels, project(): pl.pallas_call(functools.partial(project_kernel, n_tp), out_shape=jax.Sha...  32 us

profile of v3, /device:TPU:0, one launch (start us, length us, event | category | flops | bytes accessed | tf_op | source)
XLA Modules:
  0.0 99.7 jit_solution(7402745414806540262)
XLA Ops:
  0.0 32.0 %gather_project.1.qkv_ref = bf16[256,1536]{1,0:T(8,128)(2,1)} custom-call(bf16[64,8192]{1,0:T(8,128)(2,1)} %x_ref.3, bf16[8192]{0:T(1024)(128)(2,1)} %gain_ref.2, bf16[8192,1024]{1,0:T(8,128)(2,1)} %wq_ref.1, bf16[8192,256]{1,0:T(8,128)(2,1)} %wk_ref.1, bf16[8192,256]{1,0:T(8,128)(2,1)} %wv_ref.1), custom_call_target="tpu_custom_call" | custom-call | tf_op jit(solution)/shard_map/gather_project/pallas_call | solution.py:213
  32.0 66.1 %attend_talk.1 = bf16[320,256]{1,0:T(8,128)(2,1)} custom-call(bf16[256,1536]{1,0:T(8,128)(2,1)} %gather_project.1.qkv_ref, bf16[16,320,256]{2,1,0:T(8,128)(2,1)} %ck_ref.1, bf16[16,320,256]{2,1,0:T(8,128)(2,1)} %cv_ref.1, s32[1,256]{1,0:T(1,128)} %ids_ref.1, s32[1,16]{1,0:T(1,128)} %lens_ref.1, s32[1,16]{1,0:T(1,128)} %bitcast.1, bf16[1024,8192]{1,0:T(8,128)(2,1)} %wo_ref.1, ...), custom_call_target="tpu_custom_call" | custom-call | tf_op jit(solution)/shard_map/attend_talk/pallas_call | solution.py:554
  98.1 1.6 %copy.15 = bf16[320,256]{1,0:T(8,128)(2,1)} copy(bf16[320,256]{1,0:T(8,128)(2,1)} %attend_talk.1) | data formatting | bytes 327680
